TPU v7x, 32 devices: a whole 2x2x4 slice. The times are simulated.
32 devices in a mesh: dp: 8 (over z, y), mp: 4 (over x, core).
Axes of the slice: x: 2, y: 2, z: 4, core: 2. Of those that a mesh axis runs over, the one named last changes fastest.
Arguments:
- tokens: bfloat16 [1536, 1152], P('dp'), may hold values from -6 to 6
- doc_lengths: int32 [16, 2], P('dp'), may hold values from 1 to 48, as said below
- cotangent: bfloat16 [1536, 1152], P('dp'), may hold values from -6 to 6
- query_weight: bfloat16 [1152, 1024], P('dp', 'mp'), may hold values from -0.1875 to 0.1875
- key_weight: bfloat16 [1152, 256], P('dp'), may hold values from -0.1875 to 0.1875
- value_weight: bfloat16 [1152, 256], P('dp'), may hold values from -0.1875 to 0.1875
- out_weight: bfloat16 [1024, 1152], P('mp', 'dp'), may hold values from -0.1875 to 0.1875
- gate_weight: bfloat16 [1152, 6912], P('dp', 'mp'), may hold values from -0.1875 to 0.1875
- up_weight: bfloat16 [1152, 6912], P('dp', 'mp'), may hold values from -0.1875 to 0.1875
- down_weight: bfloat16 [6912, 1152], P('mp', 'dp'), may hold values from -0.078125 to 0.078125
- pre_attn_gain: bfloat16 [1152], P('dp'), may hold values from 0.5 to 1.5
- post_attn_gain: bfloat16 [1152], P('dp'), may hold values from 0.5 to 1.5
- pre_ffn_gain: bfloat16 [1152], P('dp'), may hold values from 0.5 to 1.5
- post_ffn_gain: bfloat16 [1152], P('dp'), may hold values from 0.5 to 1.5
- query_gain: bfloat16 [256], P('dp'), may hold values from 0.5 to 1.5
- key_gain: bfloat16 [256], P('dp'), may hold values from 0.5 to 1.5
Outputs:
- mixed: bfloat16 [1536, 1152], P('dp')
- tokens_grad: float32 [1536, 1152], P('dp')
- query_grad: float32 [1152, 1024], P('dp', 'mp')
- key_grad: float32 [1152, 256], P('dp')
- value_grad: float32 [1152, 256], P('dp')
- out_grad: float32 [1024, 1152], P('mp', 'dp')
- gate_grad: float32 [1152, 6912], P('dp', 'mp')
- up_grad: float32 [1152, 6912], P('dp', 'mp')
- down_grad: float32 [6912, 1152], P('mp', 'dp')
- pre_attn_grad: float32 [1152], P('dp')
- post_attn_grad: float32 [1152], P('dp')
- pre_ffn_grad: float32 [1152], P('dp')
- post_ffn_grad: float32 [1152], P('dp')
- query_gain_grad: float32 [256], P('dp')
- key_gain_grad: float32 [256], P('dp')
Inputs may be any that keep to these rules, and one draw needn't show every extreme that they name: Row b of doc_lengths gives the 2 document lengths of buffer b, the buffers of one index of dp being 2 consecutive rows; the documents lie end to end from the buffer's first row, and the rows after them are padding.
All inputs are finite; a program needn't handle non-finite values.
Results may differ from a plain program's by a relative error of at most 0.019.
Values may be sent and summed in bfloat16 or wider, within the bound.
A program may use at most 128 MiB of HBM per device.

v0:
```python
import jax
import jax.numpy as jnp
from jax import lax
from jax.sharding import PartitionSpec as P

WINDOW = 512
EPSILON = 1e-06
THETA_BASE = 10000.0
NEGATIVE = -1e30


def matmul(left_op, right_op):
    return jnp.dot(left_op, right_op, preferred_element_type=jnp.float32)


def inner_rows(left_op, right_op):
    return lax.dot_general(
        left_op, right_op, (((0,), (0,)), ((), ())), preferred_element_type=jnp.float32
    )


def inner_cols(left_op, right_op):
    return lax.dot_general(
        left_op, right_op, (((1,), (1,)), ((), ())), preferred_element_type=jnp.float32
    )


def normed(values, factor):
    return values * lax.rsqrt(jnp.mean(values * values, axis=-1, keepdims=True) + EPSILON) * factor


def rotate(values, cosine, sine_table):
    half_width = values.shape[-1] // 2
    leading = values[..., :half_width]
    trailing = values[..., half_width:]
    return jnp.concatenate(
        [leading * cosine - trailing * sine_table, trailing * cosine + leading * sine_table],
        axis=-1,
    )


def layout(lengths, row_count):
    batches, docs = lengths.shape
    total = batches * row_count
    index = jnp.arange(total, dtype=jnp.int32)
    buffer = index // row_count
    inside = index % row_count
    order = jnp.arange(docs, dtype=jnp.int32)
    ends = jnp.sum(
        jnp.where(order[None, :, None] >= order[None, None, :], lengths[:, None, :], 0), axis=2
    )
    row_ends = jnp.repeat(ends, row_count, axis=0)
    row_lengths = jnp.repeat(lengths, row_count, axis=0)
    passed = inside[:, None] >= row_ends
    segment = jnp.sum(passed.astype(jnp.int32), axis=1)
    begins = jnp.sum(jnp.where(passed, row_lengths, 0), axis=1)
    position = inside - begins
    live_rows = (segment < docs).astype(jnp.float32)
    group = buffer * (docs + 1) + segment
    allowed = (
        (group[:, None] == group[None, :])
        & (index[None, :] <= index[:, None])
        & (index[:, None] - index[None, :] < WINDOW)
    )
    return (position, live_rows, allowed)


def angles(position, head_width):
    half_width = head_width // 2
    frequency = THETA_BASE ** (-2.0 * jnp.arange(half_width, dtype=jnp.float32) / head_width)
    turned = position.astype(jnp.float32)[:, None] * frequency[None, :]
    return (jnp.cos(turned), jnp.sin(turned))


def on_device(
    tokens,
    doc_lengths,
    cotangent,
    query_weight,
    key_weight,
    value_weight,
    out_weight,
    gate_weight,
    up_weight,
    down_weight,
    pre_attn_gain,
    post_attn_gain,
    pre_ffn_gain,
    post_ffn_gain,
    query_gain,
    key_gain,
):
    low = jnp.bfloat16
    full = jnp.float32
    dp = lax.axis_size("dp")
    mp = lax.axis_size("mp")
    shard = lax.axis_index("mp")
    rows, width = tokens.shape
    share = width // dp
    head_width = query_weight.shape[1]
    units = gate_weight.shape[1] // dp
    own_rows = rows // mp
    own = (shard * own_rows, own_rows)
    gain_head = query_gain.shape[0]
    gains = jnp.concatenate(
        [pre_attn_gain, post_attn_gain, pre_ffn_gain, post_ffn_gain, query_gain, key_gain]
    )
    block = jnp.concatenate([query_weight, key_weight, value_weight, out_weight.T], axis=1)
    gains_row = jnp.pad(gains, (0, block.shape[1] - gains.shape[0]))[None]
    packed = jnp.concatenate([block, jnp.pad(gains_row, ((0, 15), (0, 0)))], axis=0)
    packed = lax.all_gather(packed, "dp", axis=0, tiled=False)
    attn_w = packed[:, :share].reshape(width, 4 * head_width)
    qkv_w = attn_w[:, : 3 * head_width]
    out_wt = attn_w[:, 3 * head_width :]
    all_gains = packed[:, share].astype(full)
    gain_one, gain_two, gain_three, gain_four = (
        all_gains[:, i * share : (i + 1) * share].reshape(width) for i in range(4)
    )
    query_g = all_gains[:, 4 * share : 4 * share + gain_head].reshape(head_width)
    key_g = all_gains[:, 4 * share + gain_head : 4 * share + 2 * gain_head].reshape(head_width)
    ffn_block = jnp.stack([gate_weight, up_weight, down_weight.T], axis=0)
    ffn_block = ffn_block.reshape(3, share, dp, units).transpose(2, 1, 0, 3)
    ffn_block = ffn_block.reshape(dp, share, 3 * units)
    ffn_w = lax.all_to_all(ffn_block, "dp", split_axis=0, concat_axis=0, tiled=True)
    ffn_w = ffn_w.reshape(width, 3 * units)
    glu_w = ffn_w[:, : 2 * units]
    down_wt = ffn_w[:, 2 * units :]
    inputs = tokens.astype(full)
    position, live_rows, allowed = layout(doc_lengths, rows // doc_lengths.shape[0])
    cosine, sine_table = angles(position, head_width)
    normed_in = normed(inputs, gain_one).astype(low)
    projected = matmul(normed_in, qkv_w)
    query_pre = projected[:, :head_width]
    key_pre = projected[:, head_width : 2 * head_width]
    value_low = projected[:, 2 * head_width :].astype(low)
    query_low = rotate(normed(query_pre, query_g), cosine, sine_table).astype(low)
    key_low = rotate(normed(key_pre, key_g), cosine, sine_table).astype(low)
    score_scale = head_width ** (-0.5)
    scores = inner_cols(query_low, key_low) * score_scale
    scores = jnp.where(allowed, scores, NEGATIVE)
    row_peak = jnp.max(scores, axis=1, keepdims=True)
    raised = jnp.exp(scores - row_peak)
    attention = raised / jnp.sum(raised, axis=1, keepdims=True)
    attention_low = attention.astype(low)
    attended = matmul(attention_low, value_low).astype(low)
    attn_part = inner_cols(attended, out_wt).astype(low)
    attn_sum = lax.psum_scatter(attn_part, "mp", scatter_dimension=0, tiled=True).astype(full)
    inputs_own = lax.dynamic_slice_in_dim(tokens, *own, axis=0).astype(full)
    upstream = lax.dynamic_slice_in_dim(cotangent, *own, axis=0).astype(full)
    live = lax.dynamic_slice_in_dim(live_rows, *own, axis=0)[:, None]

    def post_norm(values, factor):
        return normed(values, factor) * live

    attn_out, back_two = jax.vjp(post_norm, attn_sum, gain_two)
    middle = inputs_own + attn_out
    normed_mid_own, back_three = jax.vjp(normed, middle, gain_three)
    normed_mid = lax.all_gather(normed_mid_own.astype(low), ("dp", "mp"), axis=0, tiled=True)
    glu_pre = matmul(normed_mid, glu_w)
    gate_proj = glu_pre[:, :units]
    up_proj = glu_pre[:, units:]

    def glu(gate_in, up_in):
        return jax.nn.gelu(gate_in, approximate=True) * up_in

    hidden_full, back_glu = jax.vjp(glu, gate_proj, up_proj)
    hidden = hidden_full.astype(low)
    ffn_part = inner_cols(hidden, down_wt).astype(low)
    ffn_sum = lax.psum_scatter(ffn_part, ("dp", "mp"), scatter_dimension=0, tiled=True).astype(full)
    ffn_out, back_four = jax.vjp(post_norm, ffn_sum, gain_four)
    mixed_own = (middle + ffn_out).astype(low)
    d_ffn_own, grad_four = back_four(upstream)
    d_ffn = lax.all_gather(d_ffn_own.astype(low), ("dp", "mp"), axis=0, tiled=True)
    grad_down_t = inner_rows(d_ffn, hidden)
    d_hidden = matmul(d_ffn, down_wt)
    d_gate, d_up = back_glu(d_hidden)
    d_glu = jnp.concatenate([d_gate.astype(low), d_up.astype(low)], axis=1)
    d_mid_part = inner_cols(d_glu, glu_w).astype(low)
    d_mid = lax.psum_scatter(d_mid_part, ("dp", "mp"), scatter_dimension=0, tiled=True).astype(full)
    grad_glu = inner_rows(normed_mid, d_glu)
    ffn_grad = jnp.concatenate([grad_glu, grad_down_t], axis=1).astype(low)
    ffn_grad = ffn_grad.reshape(dp, share, 3 * units)
    ffn_grad = lax.all_to_all(ffn_grad, "dp", split_axis=0, concat_axis=0, tiled=True)
    ffn_grad = ffn_grad.reshape(dp, share, 3, units).transpose(2, 1, 0, 3)
    ffn_grad = ffn_grad.reshape(3, share, dp * units).astype(full)
    d_mid_add, grad_three = back_three(d_mid)
    d_middle = upstream + d_mid_add
    d_attn_own, grad_two = back_two(d_middle)
    d_attn = lax.all_gather(d_attn_own.astype(low), "mp", axis=0, tiled=True)
    grad_out_t = inner_rows(d_attn, attended)
    d_attended = matmul(d_attn, out_wt).astype(low)
    d_value = inner_rows(attention_low, d_attended).astype(low)
    d_probs = inner_cols(d_attended, value_low)
    d_scores = attention * (d_probs - jnp.sum(attention * d_probs, axis=1, keepdims=True))
    d_scores = d_scores.astype(low)
    d_query_rot = matmul(d_scores, key_low) * score_scale
    d_key_rot = inner_rows(d_scores, query_low) * score_scale

    def turned(values, factor):
        return rotate(normed(values, factor), cosine, sine_table)

    _, back_query = jax.vjp(turned, query_pre, query_g)
    d_query_pre, grad_qgain = back_query(d_query_rot)
    _, back_key = jax.vjp(turned, key_pre, key_g)
    d_key_pre, grad_kgain = back_key(d_key_rot)
    d_qkv = jnp.concatenate([d_query_pre.astype(low), d_key_pre.astype(low), d_value], axis=1)
    d_in_part = inner_cols(d_qkv, qkv_w).astype(low)
    d_in = lax.psum_scatter(d_in_part, "mp", scatter_dimension=0, tiled=True).astype(full)
    grad_qkv = inner_rows(normed_in, d_qkv)
    _, back_one = jax.vjp(normed, inputs_own, gain_one)
    d_in_add, grad_one = back_one(d_in)
    tokens_grad_own = d_middle + d_in_add
    pieces = [
        g.reshape(dp, -1)
        for g in (grad_one, grad_two, grad_three, grad_four, grad_qgain, grad_kgain)
    ]
    gains_grad = jnp.concatenate(pieces, axis=1)
    gains_grad = jnp.pad(gains_grad, ((0, 0), (0, 4 * head_width - gains_grad.shape[1])))
    weights_grad = jnp.concatenate([grad_qkv, grad_out_t], axis=1).reshape(
        dp, share, 4 * head_width
    )
    owned = jnp.concatenate(
        [weights_grad, jnp.pad(gains_grad[:, None], ((0, 0), (0, 15), (0, 0)))], axis=1
    ).astype(low)
    owned = lax.psum_scatter(owned, "dp", scatter_dimension=0, tiled=True)[0].astype(full)
    shared = jnp.concatenate(
        [
            owned[:share, head_width : 3 * head_width].reshape(-1),
            owned[share, : 4 * share + 2 * gain_head],
        ]
    )
    shared = lax.psum(shared, "mp")
    kv_grad = shared[: 2 * share * head_width].reshape(share, 2 * head_width)
    gain_out = shared[2 * share * head_width :]
    mixed = lax.all_gather(mixed_own, "mp", axis=0, tiled=True)
    tokens_grad = lax.all_gather(tokens_grad_own.astype(low), "mp", axis=0, tiled=True).astype(full)
    return (
        mixed,
        tokens_grad,
        owned[:share, :head_width],
        kv_grad[:, :head_width],
        kv_grad[:, head_width:],
        owned[:share, 3 * head_width :].T,
        ffn_grad[0],
        ffn_grad[1],
        ffn_grad[2].T,
        gain_out[:share],
        gain_out[share : 2 * share],
        gain_out[2 * share : 3 * share],
        gain_out[3 * share : 4 * share],
        gain_out[4 * share : 4 * share + gain_head],
        gain_out[4 * share + gain_head :],
    )


def solution(mesh):
    placed = (
        P("dp", None),
        P("dp", None),
        P("dp", None),
        P("dp", "mp"),
        P("dp", None),
        P("dp", None),
        P("mp", "dp"),
        P("dp", "mp"),
        P("dp", "mp"),
        P("mp", "dp"),
        P("dp"),
        P("dp"),
        P("dp"),
        P("dp"),
        P("dp"),
        P("dp"),
    )
    return jax.shard_map(
        on_device,
        mesh=mesh,
        in_specs=placed,
        out_specs=(
            P("dp", None),
            P("dp", None),
            P("dp", "mp"),
            P("dp", None),
            P("dp", None),
            P("mp", "dp"),
            P("dp", "mp"),
            P("dp", "mp"),
            P("mp", "dp"),
            P("dp"),
            P("dp"),
            P("dp"),
            P("dp"),
            P("dp"),
            P("dp"),
        ),
        check_vma=False,
    )
```

profile of v0, /device:TPU:0, one launch (start us, length us, event | category | flops | bytes accessed | tf_op | source)
XLA Modules:
  0.0 653.2 jit_solution(11283578642979378089)
XLA Ops:
  7.2 4.1 concatenate.49
  16.2 54.4 %all-gather.9.cloned.1.call-done = bf16[1280,1024]{1,0:T(8,128)(2,1)} async-done(((bf16[160,1024]{1,0:T(8,128)(2,1)}), bf16[1280,1024]{1,0:T(8,128)(2,1)}) %all-gather.9.cloned.1.call-update) | async-done | bytes 2621456 | tf_op jit(solution)/shard_map/all_gather | solution.py:111
  80.0 19.5 %reduce-scatter.6.cloned.1.call-done = bf16[48,1152]{1,0:T(8,128)(2,1)} async-done(((bf16[192,1152]{1,0:T(8,128)(2,1)}), bf16[48,1152]{1,0:T(8,128)(2,1)}) %reduce-scatter.6.cloned.1.call-update) | async-done | bytes 110608 | tf_op jit(solution)/shard_map/reduce_scatter | solution.py:147
  111.2 4.4 maximum_bitcast_fusion
  115.6 3.1 reshape.329
  118.8 61.1 %all_to_all.10 = bf16[8,144,648]{2,1,0:T(8,128)(2,1)S(1)} all-to-all(bf16[8,144,648]{2,1,0:T(8,128)(2,1)} %reshape.329), channel_id=1, replica_groups=mesh['dp'=8,'mp'=4] {'dp'}, dimensions={0} | all-to-all | bytes 2985984 | tf_op jit(solution)/shard_map/all_to_all | solution.py:124
  179.8 4.0 fusion.14
  185.8 3.3 convolution_convert_fusion
  189.9 100.5 %reduce-scatter.8.cloned.1.call-done = bf16[48,1152]{1,0:T(8,128)(2,1)} async-done(((bf16[1536,1152]{1,0:T(8,128)(2,1)}), bf16[48,1152]{1,0:T(8,128)(2,1)}) %reduce-scatter.8.cloned.1.call-update) | async-done | bytes 110608 | tf_op jit(solution)/shard_map/reduce_scatter | solution.py:169
  294.4 59.1 %all-gather.7.cloned.1.call-done = bf16[1536,1152]{1,0:T(8,128)(2,1)} async-done(((bf16[48,1152]{1,0:T(8,128)(2,1)}), bf16[1536,1152]{1,0:T(8,128)(2,1)}) %all-gather.7.cloned.1.call-update) | async-done | bytes 3538960 | tf_op jit(solution)/shard_map/all_gather | solution.py:173
  353.5 5.0 fusion.11
  359.3 4.2 convolution_convert_fusion.1
  363.8 101.8 %reduce-scatter.10.cloned.1.call-done = bf16[48,1152]{1,0:T(8,128)(2,1)} async-done(((bf16[1536,1152]{1,0:T(8,128)(2,1)}), bf16[48,1152]{1,0:T(8,128)(2,1)}) %reduce-scatter.10.cloned.1.call-update) | async-done | bytes 110608 | tf_op jit(solution)/shard_map/reduce_scatter | solution.py:179
  469.0 6.8 %all_gather.26 = bf16[192,1152]{1,0:T(8,128)(2,1)S(1)} all-gather(bf16[48,1152]{1,0:T(8,128)(2,1)S(1)} %fusion.45), channel_id=1, replica_groups=mesh['dp'=8,'mp'=4] {'mp'}, dimensions={0}, use_global_device_ids=true | all-gather | bytes 552960 | tf_op jit(solution)/shard_map/all_gather | solution.py:189
  485.4 2.9 copy.63
  488.3 11.8 %reduce-scatter.12.cloned.1.call-done = bf16[48,1152]{1,0:T(8,128)(2,1)} async-done(((bf16[192,1152]{1,0:T(8,128)(2,1)}), bf16[48,1152]{1,0:T(8,128)(2,1)}) %reduce-scatter.12.cloned.1.call-update) | async-done | bytes 110608 | tf_op jit(solution)/shard_map/reduce_scatter | solution.py:208
  503.4 3.1 convolution_convert_fusion.5
  506.7 4.1 convolution_convert_fusion.3
  512.1 61.5 %all_to_all.11 = bf16[8,144,648]{2,1,0:T(8,128)(2,1)S(1)} all-to-all(bf16[8,144,648]{2,1,0:T(8,128)(2,1)S(1)} %pad_maximum_fusion.1), channel_id=1, replica_groups=mesh['dp'=8,'mp'=4] {'dp'}, dimensions={0} | all-to-all | bytes 2985984 | tf_op jit(solution)/shard_map/all_to_all | solution.py:183
  573.6 4.9 reshape.342
  578.4 8.8 %fusion.116 = (f32[1,144,8,216]{3,0,1,2:T(1,128)S(1)}, f32[1,144,8,216]{3,0,1,2:T(1,128)S(1)}, f32[1,144,8,216]{3,0,1,2:T(1,128)S(1)}) fusion(f32[3,144,8,216]{3,0,1,2:T(4,128)} %bitcast.45), kind=kLoop, calls=%fused_computation.220 | loop fusion | bytes 5971968 | tf_op jit(solution)/shard_map/slice | solution.py:246
  593.6 6.7 %all_gather.24 = bf16[192,1152]{1,0:T(8,128)(2,1)S(1)} all-gather(bf16[48,1152]{1,0:T(8,128)(2,1)S(1)} %copy-done.18), channel_id=1, replica_groups=mesh['dp'=8,'mp'=4] {'mp'}, dimensions={0}, use_global_device_ids=true | all-gather | bytes 552960 | tf_op jit(solution)/shard_map/all_gather | solution.py:235
  601.4 6.8 %all_gather.27 = bf16[192,1152]{1,0:T(8,128)(2,1)S(1)} all-gather(bf16[48,1152]{1,0:T(8,128)(2,1)S(1)} %fusion.47), channel_id=1, replica_groups=mesh['dp'=8,'mp'=4] {'mp'}, dimensions={0}, use_global_device_ids=true | all-gather | bytes 552960 | tf_op jit(solution)/shard_map/all_gather | solution.py:236
  611.9 29.4 %all-reduce.10.cloned.1.call-done = f32[74368]{0:T(1024)} async-done(((f32[74368]{0:T(1024)}), f32[74368]{0:T(1024)}) %all-reduce.10.cloned.1.call-update) | async-done | bytes 297488 | tf_op jit(solution)/shard_map/psum | solution.py:232
  (271 shorter events, 66.8 us)
Async XLA Ops:
  7.2 63.4 %all-gather.9.cloned.1.call-start = ((), (), s32[]{:S(2)}) async-start(), calls=%async_computation.15 | async-start | bytes 2949120 | tf_op jit(solution)/shard_map/all_gather | solution.py:111
  13.1 86.4 %reduce-scatter.6.cloned.1.call-start = ((), (), s32[]{:S(2)}) async-start(), calls=%async_computation.7 | async-start | bytes 552960 | tf_op jit(solution)/shard_map/reduce_scatter | solution.py:147
  15.0 60.9 %copy-start.57 = (f32[128]{0:T(128)}, f32[128]{0:T(128)S(1)}, u32[]{:S(2)}) copy-start(f32[128]{0:T(128)S(1)} %multiply_power_fusion) | copy-start | bytes 1540
  16.2 58.7 %copy-start.59 = (f32[192]{0:T(256)}, f32[192]{0:T(256)S(1)}, u32[]{:S(2)}) copy-start(f32[192]{0:T(256)S(1)} %add_rsqrt_fusion) | copy-start | bytes 2308
  16.2 59.7 %copy-start.45 = (f32[192]{0:T(256)}, f32[192]{0:T(256)S(1)}, u32[]{:S(2)}) copy-start(f32[192]{0:T(256)S(1)} %fusion.98) | copy-start | bytes 2308
  79.7 100.1 %all-gather.5.cloned.1.call-start = ((), (), s32[]{:S(2)}) async-start(), calls=%async_computation.8 | async-start | bytes 3649536 | tf_op jit(solution)/shard_map/all_gather | solution.py:158
  104.1 186.4 %reduce-scatter.8.cloned.1.call-start = ((), (), s32[]{:S(2)}) async-start(), calls=%async_computation.9 | async-start | bytes 3649536 | tf_op jit(solution)/shard_map/reduce_scatter | solution.py:169
  189.1 102.3 %copy-start.21 = (bf16[192,1152]{1,0:T(8,128)(2,1)S(1)}, bf16[192,1152]{1,0:T(8,128)(2,1)}, u32[]{:S(2)}) copy-start(bf16[192,1152]{1,0:T(8,128)(2,1)} %param.18) | copy-start | bytes 1327108
  189.1 102.3 %copy-start.34 = (f32[48]{0:T(128)S(1)}, f32[48]{0:T(128)}, u32[]{:S(2)}) copy-start(f32[48]{0:T(128)} %copy-done.33) | copy-start | bytes 580
  189.1 164.3 %all-gather.7.cloned.1.call-start = ((), (), s32[]{:S(2)}) async-start(), calls=%async_computation.10 | async-start | bytes 3649536 | tf_op jit(solution)/shard_map/all_gather | solution.py:173
  294.4 171.2 %reduce-scatter.10.cloned.1.call-start = ((), (), s32[]{:S(2)}) async-start(), calls=%async_computation.11 | async-start | bytes 3649536 | tf_op jit(solution)/shard_map/reduce_scatter | solution.py:179
  363.5 102.0 %copy-start.3 = (bf16[48,1152]{1,0:T(8,128)(2,1)S(1)}, bf16[48,1152]{1,0:T(8,128)(2,1)}, u32[]{:S(2)}) copy-start(bf16[48,1152]{1,0:T(8,128)(2,1)} %reduce-scatter.6.cloned.1.call-done) | copy-start | bytes 331780
  363.5 102.0 %copy-start.44 = (f32[48]{0:T(128)S(1)}, f32[48]{0:T(128)}, u32[]{:S(2)}) copy-start(f32[48]{0:T(128)} %copy-done.43) | copy-start | bytes 580
  363.5 102.0 %copy-start.52 = (f32[48]{0:T(128)S(1)}, f32[48]{0:T(128)}, u32[]{:S(2)}) copy-start(f32[48]{0:T(128)} %copy-done.51) | copy-start | bytes 580
  363.5 103.3 %copy-start.66 = (f32[48]{0:T(128)S(1)}, f32[48]{0:T(128)}, u32[]{:S(2)}) copy-start(f32[48]{0:T(128)} %copy-done.65) | copy-start | bytes 580
  363.5 103.3 %copy-start.11 = (bf16[48,1152]{1,0:T(8,128)(2,1)S(1)}, bf16[48,1152]{1,0:T(8,128)(2,1)}, u32[]{:S(2)}) copy-start(bf16[48,1152]{1,0:T(8,128)(2,1)} %reduce-scatter.8.cloned.1.call-done) | copy-start | bytes 331780
  363.6 105.3 %copy-start.64 = (f32[48]{0:T(128)S(1)}, f32[48]{0:T(128)}, u32[]{:S(2)}) copy-start(f32[48]{0:T(128)} %copy-done.63) | copy-start | bytes 580
  363.6 112.3 %copy-start.5 = (bf16[8,144,1024]{2,1,0:T(8,128)(2,1)S(1)}, bf16[8,144,1024]{2,1,0:T(8,128)(2,1)}, u32[]{:S(2)}) copy-start(bf16[8,144,1024]{2,1,0:T(8,128)(2,1)} %copy-done.4) | copy-start | bytes 7077892
  363.6 136.5 %reduce-scatter.12.cloned.1.call-start = ((), (), s32[]{:S(2)}) async-start(), calls=%async_computation.12 | async-start | bytes 552960 | tf_op jit(solution)/shard_map/reduce_scatter | solution.py:208
  363.7 112.5 %copy-start.13 = (f32[192,192]{0,1:T(8,128)S(1)}, f32[192,192]{0,1:T(8,128)}, u32[]{:S(2)}) copy-start(f32[192,192]{0,1:T(8,128)} %copy-done.12) | copy-start | bytes 442372
  363.7 112.5 %copy-start.54 = (f32[192]{0:T(256)S(1)}, f32[192]{0:T(256)}, u32[]{:S(2)}) copy-start(f32[192]{0:T(256)} %copy-done.53) | copy-start | bytes 2308
  363.8 112.5 %copy-start.56 = (f32[192]{0:T(256)S(1)}, f32[192]{0:T(256)}, u32[]{:S(2)}) copy-start(f32[192]{0:T(256)} %copy-done.55) | copy-start | bytes 2308
  479.9 129.4 %reduce-scatter.14.cloned.1.call-start = ((), (), s32[]{:S(2)}) async-start(), calls=%async_computation.13 | async-start | bytes 2949120 | tf_op jit(solution)/shard_map/reduce_scatter | solution.py:225
  503.3 138.0 %all-reduce.10.cloned.1.call-start = ((), (), s32[]{:S(2)}) async-start(), calls=%async_computation.14 | async-start | bytes 598016 | tf_op jit(solution)/shard_map/psum | solution.py:232
  (56 other events, 195.3 us)
Sparse Core Ops, SparseCore 0:
  13.2 57.3 all-gather.8
  79.8 19.6 reduce-scatter.5
  104.2 70.9 all-gather.4
  189.3 101.1 reduce-scatter.7
  294.5 58.9 all-gather.6
  363.7 101.7 reduce-scatter.9
  480.0 20.0 reduce-scatter.11
  503.6 93.4 reduce-scatter.13
  611.3 29.9 all-reduce.9
where the time goes:
time: 654 us; the launch traced here: 653 us
  waiting for transfers between devices  377 us (58%)
  blocking collectives  143 us (22%)
  local copies, waits for them, and re-layouts  54 us (8%)
  other arithmetic  32.3 us (5%)
  matrix products  31.6 us (5%)
  between operations  15.1 us (2%)
    reduce_scatter x1, waiting for transfers between devices, on_device(): lax.psum_scatter(d_mid_part, ('dp', 'mp'), scatter_dimension=0, tiled=True)  102 us
    reduce_scatter x1, waiting for transfers between devices, on_device(): lax.psum_scatter(ffn_part, ('dp', 'mp'), scatter_dimension=0, tiled=True)  101 us
    all_to_all x1, blocking collectives, on_device(): lax.all_to_all(ffn_grad, 'dp', split_axis=0, concat_axis=0, tiled=True)  61.5 us
    all_to_all x1, blocking collectives, on_device(): lax.all_to_all(ffn_block, 'dp', split_axis=0, concat_axis=0, tiled=True)  61.1 us
    all_gather x1, waiting for transfers between devices, on_device(): lax.all_gather(d_ffn_own.astype(low), ('dp', 'mp'), axis=0, tiled=True)  59.1 us
    all_gather x1, waiting for transfers between devices, on_device(): packed = lax.all_gather(packed, 'dp', axis=0, tiled=False)  54.4 us
    psum x1, waiting for transfers between devices, on_device(): shared = lax.psum(shared, 'mp')  29.4 us
    reduce_scatter x1, waiting for transfers between devices, on_device(): lax.psum_scatter(attn_part, 'mp', scatter_dimension=0, tiled=True)  19.5 us
  transfers between devices with their start and end apart: 9, of which 7 were waited for; matrix products, arithmetic and copies ran while one was open for 9% of the time, Pallas kernels for 0%

commit v1 on v0

--- a/solution.py
+++ b/solution.py
@@ -229,7 +229,8 @@
             owned[share, : 4 * share + 2 * gain_head],
         ]
     )
-    shared = lax.psum(shared, "mp")
+    blocks = lax.all_gather(shared, "mp", axis=0, tiled=False)
+    shared = blocks.sum(axis=0)
     kv_grad = shared[: 2 * share * head_width].reshape(share, 2 * head_width)
     gain_out = shared[2 * share * head_width :]
     mixed = lax.all_gather(mixed_own, "mp", axis=0, tiled=True)

time: 654 us -> 654 us (level); the launches traced: 653 us -> 645 us
  waiting for transfers between devices: 377 us -> 366 us
    psum x1 -> x0, waiting for transfers between devices: 29.4 us -> none  [on_device(): shared = lax.psum(shared, 'mp')]
    reduce_scatter x1, waiting for transfers between devices: 0.01 us -> 18.8 us  [on_device(): lax.psum_scatter(owned, 'dp', scatter_dimension=0, tiled=True)[0]]
where the time goes in v1:
time: 654 us; the launch traced here: 645 us
  waiting for transfers between devices  366 us (56%)
  blocking collectives  143 us (22%)
  local copies, waits for them, and re-layouts  54.2 us (8%)
  other arithmetic  34 us (5%)
  matrix products  31.6 us (5%)
  between operations  15.5 us (2%)
    reduce_scatter x1, waiting for transfers between devices, on_device(): lax.psum_scatter(d_mid_part, ('dp', 'mp'), scatter_dimension=0, tiled=True)  102 us
    reduce_scatter x1, waiting for transfers between devices, on_device(): lax.psum_scatter(ffn_part, ('dp', 'mp'), scatter_dimension=0, tiled=True)  100 us
    all_to_all x1, blocking collectives, on_device(): lax.all_to_all(ffn_grad, 'dp', split_axis=0, concat_axis=0, tiled=True)  61.5 us
    all_to_all x1, blocking collectives, on_device(): lax.all_to_all(ffn_block, 'dp', split_axis=0, concat_axis=0, tiled=True)  61.2 us
    all_gather x1, waiting for transfers between devices, on_device(): lax.all_gather(d_ffn_own.astype(low), ('dp', 'mp'), axis=0, tiled=True)  59.2 us
    all_gather x1, waiting for transfers between devices, on_device(): packed = lax.all_gather(packed, 'dp', axis=0, tiled=False)  54.4 us
    reduce_scatter x1, waiting for transfers between devices, on_device(): lax.psum_scatter(attn_part, 'mp', scatter_dimension=0, tiled=True)  19.5 us
    reduce_scatter x1, waiting for transfers between devices, on_device(): lax.psum_scatter(owned, 'dp', scatter_dimension=0, tiled=True)[0]  18.8 us
  transfers between devices with their start and end apart: 9, of which 7 were waited for; matrix products, arithmetic and copies ran while one was open for 9% of the time, Pallas kernels for 0%

profile of v1, /device:TPU:0, one launch (start us, length us, event | category | flops | bytes accessed | tf_op | source)
XLA Modules:
  0.0 644.9 jit_solution(16953379042739848265)
XLA Ops:
  7.2 4.1 concatenate.49
  16.2 54.4 %all-gather.12.cloned.1.call-done = bf16[1280,1024]{1,0:T(8,128)(2,1)} async-done(((bf16[160,1024]{1,0:T(8,128)(2,1)}), bf16[1280,1024]{1,0:T(8,128)(2,1)}) %all-gather.12.cloned.1.call-update) | async-done | bytes 2621456 | tf_op jit(solution)/shard_map/all_gather | solution.py:111
  80.0 19.5 %reduce-scatter.6.cloned.1.call-done = bf16[48,1152]{1,0:T(8,128)(2,1)} async-done(((bf16[192,1152]{1,0:T(8,128)(2,1)}), bf16[48,1152]{1,0:T(8,128)(2,1)}) %reduce-scatter.6.cloned.1.call-update) | async-done | bytes 110608 | tf_op jit(solution)/shard_map/reduce_scatter | solution.py:147
  111.1 4.4 maximum_bitcast_fusion
  115.6 3.1 reshape.329
  118.7 61.2 %all_to_all.10 = bf16[8,144,648]{2,1,0:T(8,128)(2,1)S(1)} all-to-all(bf16[8,144,648]{2,1,0:T(8,128)(2,1)} %reshape.329), channel_id=1, replica_groups=mesh['dp'=8,'mp'=4] {'dp'}, dimensions={0} | all-to-all | bytes 2985984 | tf_op jit(solution)/shard_map/all_to_all | solution.py:124
  179.9 4.0 fusion.14
  185.9 3.3 convolution_convert_fusion
  190.0 100.2 %reduce-scatter.8.cloned.1.call-done = bf16[48,1152]{1,0:T(8,128)(2,1)} async-done(((bf16[1536,1152]{1,0:T(8,128)(2,1)}), bf16[48,1152]{1,0:T(8,128)(2,1)}) %reduce-scatter.8.cloned.1.call-update) | async-done | bytes 110608 | tf_op jit(solution)/shard_map/reduce_scatter | solution.py:169
  294.2 59.2 %all-gather.10.cloned.1.call-done = bf16[1536,1152]{1,0:T(8,128)(2,1)} async-done(((bf16[48,1152]{1,0:T(8,128)(2,1)}), bf16[1536,1152]{1,0:T(8,128)(2,1)}) %all-gather.10.cloned.1.call-update) | async-done | bytes 3538960 | tf_op jit(solution)/shard_map/all_gather | solution.py:173
  353.4 5.0 fusion.11
  359.2 4.2 convolution_convert_fusion.1
  363.7 101.7 %reduce-scatter.10.cloned.1.call-done = bf16[48,1152]{1,0:T(8,128)(2,1)} async-done(((bf16[1536,1152]{1,0:T(8,128)(2,1)}), bf16[48,1152]{1,0:T(8,128)(2,1)}) %reduce-scatter.10.cloned.1.call-update) | async-done | bytes 110608 | tf_op jit(solution)/shard_map/reduce_scatter | solution.py:179
  468.9 6.8 %all_gather.32 = bf16[192,1152]{1,0:T(8,128)(2,1)S(1)} all-gather(bf16[48,1152]{1,0:T(8,128)(2,1)S(1)} %fusion.45), channel_id=1, replica_groups=mesh['dp'=8,'mp'=4] {'mp'}, dimensions={0}, use_global_device_ids=true | all-gather | bytes 552960 | tf_op jit(solution)/shard_map/all_gather | solution.py:189
  485.2 2.9 copy.73
  488.1 11.8 %reduce-scatter.12.cloned.1.call-done = bf16[48,1152]{1,0:T(8,128)(2,1)} async-done(((bf16[192,1152]{1,0:T(8,128)(2,1)}), bf16[48,1152]{1,0:T(8,128)(2,1)}) %reduce-scatter.12.cloned.1.call-update) | async-done | bytes 110608 | tf_op jit(solution)/shard_map/reduce_scatter | solution.py:208
  503.2 3.1 convolution_convert_fusion.5
  506.6 4.1 convolution_convert_fusion.3
  512.0 61.5 %all_to_all.11 = bf16[8,144,648]{2,1,0:T(8,128)(2,1)S(1)} all-to-all(bf16[8,144,648]{2,1,0:T(8,128)(2,1)S(1)} %pad_maximum_fusion.1), channel_id=1, replica_groups=mesh['dp'=8,'mp'=4] {'dp'}, dimensions={0} | all-to-all | bytes 2985984 | tf_op jit(solution)/shard_map/all_to_all | solution.py:183
  573.5 4.9 reshape.342
  578.3 18.8 %reduce-scatter.14.cloned.1.call-done = bf16[1,160,1024]{2,1,0:T(8,128)(2,1)} async-done(((bf16[8,160,1024]{2,1,0:T(8,128)(2,1)}), bf16[1,160,1024]{2,1,0:T(8,128)(2,1)}) %reduce-scatter.14.cloned.1.call-update) | async-done | bytes 327696 | tf_op jit(solution)/shard_map/reduce_scatter | solution.py:225
  600.1 8.9 %fusion.116 = (f32[1,144,8,216]{3,0,1,2:T(1,128)S(1)}, f32[1,144,8,216]{3,0,1,2:T(1,128)S(1)}, f32[1,144,8,216]{3,0,1,2:T(1,128)S(1)}) fusion(f32[3,144,8,216]{3,0,1,2:T(4,128)} %bitcast.45), kind=kLoop, calls=%fused_computation.220 | loop fusion | bytes 5971968 | tf_op jit(solution)/shard_map/slice | solution.py:247
  615.5 6.7 %all_gather.30 = bf16[192,1152]{1,0:T(8,128)(2,1)S(1)} all-gather(bf16[48,1152]{1,0:T(8,128)(2,1)S(1)} %copy-done.19), channel_id=1, replica_groups=mesh['dp'=8,'mp'=4] {'mp'}, dimensions={0}, use_global_device_ids=true | all-gather | bytes 552960 | tf_op jit(solution)/shard_map/all_gather | solution.py:236
  623.2 6.8 %all_gather.33 = bf16[192,1152]{1,0:T(8,128)(2,1)S(1)} all-gather(bf16[48,1152]{1,0:T(8,128)(2,1)S(1)} %fusion.47), channel_id=1, replica_groups=mesh['dp'=8,'mp'=4] {'mp'}, dimensions={0}, use_global_device_ids=true | all-gather | bytes 552960 | tf_op jit(solution)/shard_map/all_gather | solution.py:237
  (275 shorter events, 68.7 us)
Async XLA Ops:
  7.2 63.4 %all-gather.12.cloned.1.call-start = ((), (), s32[]{:S(2)}) async-start(), calls=%async_computation.14 | async-start | bytes 2949120 | tf_op jit(solution)/shard_map/all_gather | solution.py:111
  13.1 86.4 %reduce-scatter.6.cloned.1.call-start = ((), (), s32[]{:S(2)}) async-start(), calls=%async_computation.7 | async-start | bytes 552960 | tf_op jit(solution)/shard_map/reduce_scatter | solution.py:147
  15.0 60.9 %copy-start.58 = (f32[128]{0:T(128)}, f32[128]{0:T(128)S(1)}, u32[]{:S(2)}) copy-start(f32[128]{0:T(128)S(1)} %multiply_power_fusion) | copy-start | bytes 1540
  16.2 58.7 %copy-start.60 = (f32[192]{0:T(256)}, f32[192]{0:T(256)S(1)}, u32[]{:S(2)}) copy-start(f32[192]{0:T(256)S(1)} %add_rsqrt_fusion) | copy-start | bytes 2308
  16.2 59.7 %copy-start.46 = (f32[192]{0:T(256)}, f32[192]{0:T(256)S(1)}, u32[]{:S(2)}) copy-start(f32[192]{0:T(256)S(1)} %fusion.98) | copy-start | bytes 2308
  79.7 100.3 %all-gather.8.cloned.1.call-start = ((), (), s32[]{:S(2)}) async-start(), calls=%async_computation.8 | async-start | bytes 3649536 | tf_op jit(solution)/shard_map/all_gather | solution.py:158
  104.0 186.2 %reduce-scatter.8.cloned.1.call-start = ((), (), s32[]{:S(2)}) async-start(), calls=%async_computation.9 | async-start | bytes 3649536 | tf_op jit(solution)/shard_map/reduce_scatter | solution.py:169
  189.2 102.0 %copy-start.22 = (bf16[192,1152]{1,0:T(8,128)(2,1)S(1)}, bf16[192,1152]{1,0:T(8,128)(2,1)}, u32[]{:S(2)}) copy-start(bf16[192,1152]{1,0:T(8,128)(2,1)} %param.18) | copy-start | bytes 1327108
  189.2 102.0 %copy-start.35 = (f32[48]{0:T(128)S(1)}, f32[48]{0:T(128)}, u32[]{:S(2)}) copy-start(f32[48]{0:T(128)} %copy-done.34) | copy-start | bytes 580
  189.2 164.1 %all-gather.10.cloned.1.call-start = ((), (), s32[]{:S(2)}) async-start(), calls=%async_computation.10 | async-start | bytes 3649536 | tf_op jit(solution)/shard_map/all_gather | solution.py:173
  294.1 171.3 %reduce-scatter.10.cloned.1.call-start = ((), (), s32[]{:S(2)}) async-start(), calls=%async_computation.11 | async-start | bytes 3649536 | tf_op jit(solution)/shard_map/reduce_scatter | solution.py:179
  363.4 102.0 %copy-start.3 = (bf16[48,1152]{1,0:T(8,128)(2,1)S(1)}, bf16[48,1152]{1,0:T(8,128)(2,1)}, u32[]{:S(2)}) copy-start(bf16[48,1152]{1,0:T(8,128)(2,1)} %reduce-scatter.6.cloned.1.call-done) | copy-start | bytes 331780
  363.4 102.0 %copy-start.45 = (f32[48]{0:T(128)S(1)}, f32[48]{0:T(128)}, u32[]{:S(2)}) copy-start(f32[48]{0:T(128)} %copy-done.44) | copy-start | bytes 580
  363.4 102.0 %copy-start.53 = (f32[48]{0:T(128)S(1)}, f32[48]{0:T(128)}, u32[]{:S(2)}) copy-start(f32[48]{0:T(128)} %copy-done.52) | copy-start | bytes 580
  363.4 103.2 %copy-start.67 = (f32[48]{0:T(128)S(1)}, f32[48]{0:T(128)}, u32[]{:S(2)}) copy-start(f32[48]{0:T(128)} %copy-done.66) | copy-start | bytes 580
  363.4 103.3 %copy-start.12 = (bf16[48,1152]{1,0:T(8,128)(2,1)S(1)}, bf16[48,1152]{1,0:T(8,128)(2,1)}, u32[]{:S(2)}) copy-start(bf16[48,1152]{1,0:T(8,128)(2,1)} %reduce-scatter.8.cloned.1.call-done) | copy-start | bytes 331780
  363.4 105.3 %copy-start.65 = (f32[48]{0:T(128)S(1)}, f32[48]{0:T(128)}, u32[]{:S(2)}) copy-start(f32[48]{0:T(128)} %copy-done.64) | copy-start | bytes 580
  363.5 112.2 %copy-start.5 = (bf16[8,144,1024]{2,1,0:T(8,128)(2,1)S(1)}, bf16[8,144,1024]{2,1,0:T(8,128)(2,1)}, u32[]{:S(2)}) copy-start(bf16[8,144,1024]{2,1,0:T(8,128)(2,1)} %copy-done.4) | copy-start | bytes 7077892
  363.5 136.4 %reduce-scatter.12.cloned.1.call-start = ((), (), s32[]{:S(2)}) async-start(), calls=%async_computation.12 | async-start | bytes 552960 | tf_op jit(solution)/shard_map/reduce_scatter | solution.py:208
  363.6 112.4 %copy-start.14 = (f32[192,192]{0,1:T(8,128)S(1)}, f32[192,192]{0,1:T(8,128)}, u32[]{:S(2)}) copy-start(f32[192,192]{0,1:T(8,128)} %copy-done.13) | copy-start | bytes 442372
  363.6 112.4 %copy-start.55 = (f32[192]{0:T(256)S(1)}, f32[192]{0:T(256)}, u32[]{:S(2)}) copy-start(f32[192]{0:T(256)} %copy-done.54) | copy-start | bytes 2308
  363.7 112.4 %copy-start.57 = (f32[192]{0:T(256)S(1)}, f32[192]{0:T(256)}, u32[]{:S(2)}) copy-start(f32[192]{0:T(256)} %copy-done.56) | copy-start | bytes 2308
  479.7 117.5 %reduce-scatter.14.cloned.1.call-start = ((), (), s32[]{:S(2)}) async-start(), calls=%async_computation.13 | async-start | bytes 2949120 | tf_op jit(solution)/shard_map/reduce_scatter | solution.py:225
  503.2 129.5 %all-gather.14.cloned.1.call-start = ((), (), s32[]{:S(2)}) async-start(), calls=%async_computation.15 | async-start | bytes 1487360 | tf_op jit(solution)/shard_map/all_gather | solution.py:232
  (57 other events, 195.8 us)
Sparse Core Ops, SparseCore 0:
  13.2 57.3 all-gather.11
  79.8 19.6 reduce-scatter.5
  104.1 71.6 all-gather.7
  189.4 100.7 reduce-scatter.7
  294.3 59.0 all-gather.9
  363.6 101.7 reduce-scatter.9
  479.8 20.1 reduce-scatter.11
  503.4 93.6 reduce-scatter.13
  600.3 16.4 all-gather.13
